TPU v7x, 32 devices: a whole 2x2x4 slice. The times are simulated.
32 devices in a mesh: res: 8 (over z, y), dp: 4 (over x, core).
Axes of the slice: x: 2, y: 2, z: 4, core: 2. Of those that a mesh axis runs over, the one named last changes fastest.
Arguments:
- aligned_chain_features: bfloat16 [512, 256, 256], P('dp', 'res'), parts along dimension 0, may hold values from -6 to 6
- pair_representation_state: bfloat16 [1024, 256, 128], P(('dp', 'res')), parts along dimension 0, may hold values from -6 to 6
- gap_block_flags: int32 [512, 2], P('dp'), parts along dimension 0, may hold values from 0 to 1, as said below
- pair_norm_gain: float32 [128], replicated, may hold values from 0.1 to 1.9
- pair_head_weight: bfloat16 [128, 8], replicated, may hold values from -0.5 to 0.5
- horizontal_scaling_factor: float32 [256], replicated, may hold values from 0.1 to 1.9
- row_input_weight: bfloat16 [256, 1024], replicated, may hold values from -2 to 2
- horizontal_final_matrix: bfloat16 [256, 256], replicated, may hold values from -0.375 to 0.375
- vertical_scaling_factor: float32 [256], replicated, may hold values from 0.1 to 1.9
- column_input_weight: bfloat16 [256, 1024], replicated, may hold values from -2 to 2
- vertical_final_matrix: bfloat16 [256, 256], replicated, may hold values from -0.375 to 0.375
- feedforward_scaling_factor: float32 [256], replicated, may hold values from 0.1 to 1.9
- feedforward_widen_matrix: bfloat16 [256, 1024], replicated, may hold values from -0.375 to 0.375
- feedforward_shrink_matrix: bfloat16 [1024, 256], replicated, may hold values from -0.1875 to 0.1875
Outputs:
- msa_out: bfloat16 [512, 256, 256], P('dp', 'res'), parts along dimension 0
There are 4 independent parts, one for each index of `dp`. A program takes and returns all parts, laid end to end along the dimension named above; an argument that names none is the same for every part. Nothing has to cross between parts.
Inputs may be any that keep to these rules, and one draw needn't show every extreme that they name: `gap_block_flags`: row 0 holds no gap block, and every row has at least one block that is not a gap.
All inputs are finite; a program needn't handle non-finite values.
Results may differ from a plain program's by a relative error of at most 0.015.
The roundings to bfloat16 on the way count: a program that leaves them out, or rounds other values in their place, can miss the bound.
Values may be sent and summed in bfloat16 or wider, within the bound.
No kernel may reach another device: no remote copies, remote signals or barrier semaphores. Data moves between devices by JAX's collectives and lax.ppermute only.
A program may use at most 128 MiB of HBM per device.

v0:
```python
import functools

import jax
import jax.numpy as jnp
from jax import lax
from jax.experimental import pallas as pl
from jax.experimental.pallas import tpu as pltpu
from jax.sharding import PartitionSpec as P

BLOCK = 128
EPSILON = 1e-05
MASKED_SCORE = -1000000000.0
LANES = 128
SLAB = 16
F32 = jnp.float32
BF16 = jnp.bfloat16
VMEM_BYTES = 48 * 1024 * 1024


def layer_normalize(values_f, scale_gain):
    centred = values_f - jnp.mean(values_f, axis=-1, keepdims=True)
    spread = jnp.mean(centred * centred, axis=-1, keepdims=True)
    return centred * lax.rsqrt(spread + EPSILON) * scale_gain


def mm(lhs, rhs):
    return jnp.dot(lhs, rhs, preferred_element_type=F32)


def mm_nt(lhs, rhs):
    return lax.dot_general(lhs, rhs, (((1,), (1,)), ((), ())), preferred_element_type=F32)


def swap_matrix(outer, inner):
    size = outer * inner
    to = lax.broadcasted_iota(jnp.int32, (size, size), 0)
    come = lax.broadcasted_iota(jnp.int32, (size, size), 1)
    source = lax.rem(to, outer) * inner + lax.div(to, outer)
    return jnp.where(come == source, 1.0, 0.0).astype(BF16)


def bias_kernel(pair_ref, gain_ref, weight_ref, out_ref, rows_scr):
    heads, local_res, residues = out_ref.shape
    channels = pair_ref.shape[2]
    step = min(4, local_res)

    def body(i, carry):
        block = pair_ref[pl.ds(i * step, step)].reshape(step * residues, channels)
        normed = layer_normalize(block.astype(F32), gain_ref[...]).astype(BF16)
        projected = mm_nt(weight_ref[...], normed)
        for j in range(step):
            rows_scr[i * step + j] = projected[:, j * residues : (j + 1) * residues]
        return carry

    lax.fori_loop(0, local_res // step, body, 0)
    rows = rows_scr[...].reshape(local_res * heads, residues).astype(BF16)
    turned = mm(swap_matrix(local_res, heads), rows)
    out_ref[...] = turned.reshape(heads, local_res, residues).astype(BF16)


def softmax_keys(scores):
    e = jnp.exp(scores - jnp.max(scores, axis=0, keepdims=True))
    return (e * (1.0 / jnp.sum(e, axis=0, keepdims=True))).astype(BF16)


def gate_of(values):
    return 0.5 * jnp.tanh(0.5 * values) + 0.5


def stack(parts, axis):
    return parts[0] if len(parts) == 1 else jnp.concatenate(parts, axis=axis)


def row_kernel(
    low, count, gap_ref, x_ref, bias_ref, gain_ref, wqk_ref, wvg_ref, wout_ref, out_ref,
    bias_scr, q_scr, k_scr, v_scr, gate_scr, gated_scr,
):
    groups, seqs, local_res, channels = x_ref.shape
    heads = bias_ref.shape[1]
    residues = groups * local_res
    queries = groups * count
    depth = channels // heads
    per = LANES // depth
    scale = depth ** (-0.5)
    pair = 2 if seqs % 2 == 0 else 1
    zero = jnp.zeros((), BF16)

    row_at = lax.broadcasted_iota(jnp.int32, (residues, residues), 0)
    lane_at = lax.broadcasted_iota(jnp.int32, (residues, residues), 1)
    identity = jnp.where(row_at == lane_at, 1.0, 0.0).astype(BF16)
    for h in range(heads):
        bias_scr[h] = mm_nt(
            identity, bias_ref[:, h, low : low + count].reshape(queries, residues)
        )

    def dense(i, carry):
        normed, mine = [], []
        for j in range(pair):
            x = x_ref[:, pl.ds(i * pair + j, 1)].reshape(residues, channels)
            n = layer_normalize(x.astype(F32), gain_ref[...]).astype(BF16)
            normed.append(n)
            if count != local_res:
                n = n.reshape(groups, local_res, channels)[:, low : low + count]
                n = n.reshape(queries, channels)
            mine.append(n)
        normed, mine = stack(normed, 0), stack(mine, 0)
        q = (mm(mine, wqk_ref[:, :channels]) * scale).astype(BF16)
        k = mm(normed, wqk_ref[:, channels:]).astype(BF16)
        v = mm_nt(wvg_ref[:channels], normed).astype(BF16)
        gates = gate_of(mm_nt(wvg_ref[channels:], mine))
        for j in range(pair):
            s = i * pair + j
            q_scr[s] = q[j * queries : (j + 1) * queries]
            k_scr[s] = k[j * residues : (j + 1) * residues]
            v_scr[s] = v[:, j * residues : (j + 1) * residues]
            gate_scr[s] = gates[:, j * queries : (j + 1) * queries]
        return carry

    lax.fori_loop(0, seqs // pair, dense, 0)

    lane = lax.broadcasted_iota(jnp.int32, (residues, LANES), 1)
    ones = jnp.where(lane[:queries] == 0, 1.0, 0.0).astype(BF16)

    def attend(s, carry):
        gap_rows = [
            jnp.where((lane[:BLOCK] == 0) & (gap_ref[s, b] == 1), MASKED_SCORE, 0.0).astype(BF16)
            for b in range(residues // BLOCK)
        ]
        mask = stack(gap_rows, 0)
        attended = []
        for g in range(heads // per):
            lanes = slice(g * LANES, (g + 1) * LANES)
            q = jnp.concatenate([q_scr[s, :, lanes], ones], axis=1)
            for j in range(per):
                h = g * per + j
                k = jnp.where((lane >= j * depth) & (lane < (j + 1) * depth), k_scr[s, :, lanes], zero)
                scores = mm_nt(jnp.concatenate([k, mask], axis=1), q) + bias_scr[h]
                weights = softmax_keys(scores)
                attended.append(mm(v_scr[s, h * depth : (h + 1) * depth], weights))
        gated = (jnp.concatenate(attended, axis=0) * gate_scr[s]).astype(BF16)
        gated_scr[s] = gated.T
        return carry

    lax.fori_loop(0, seqs, attend, 0)

    def finish(i, carry):
        gated = gated_scr[pl.ds(i * pair, pair)].reshape(pair * queries, channels)
        update = mm(gated, wout_ref[...])
        for j in range(pair):
            s = i * pair + j
            x = x_ref[:, pl.ds(s, 1), low : low + count].reshape(queries, channels)
            result = x.astype(F32) + update[j * queries : (j + 1) * queries]
            out_ref[:, pl.ds(s, 1)] = result.astype(BF16).reshape(groups, 1, count, channels)
        return carry

    lax.fori_loop(0, seqs // pair, finish, 0)


def column_kernel(heads, turn, lows, done_parts, *refs):
    pieces, refs = refs[: len(lows)], refs[len(lows) :]
    done_refs, refs = refs[:done_parts], refs[done_parts:]
    (gap_ref, gain_ref, wqk_ref, wvg_ref, wout_ref, gain2_ref, widen_ref, shrink_ref) = refs[:8]
    (out_ref, turned_scr, q_scr, k_scr, v_scr, gate_scr, gated_scr, done_scr) = refs[8:]
    local_res, seqs, channels = turned_scr.shape
    depth = channels // heads
    per = LANES // depth
    halves = heads // per
    scale = depth ** (-0.5)
    batch = min(4, local_res)
    zero = jnp.zeros((), BF16)
    slabs = local_res // SLAB if turn else 0
    swap = swap_matrix(SLAB, SLAB)
    if not turn:
        turned_scr[...] = pieces[0][...]
    for c in range(slabs):
        g = 0
        for piece, low in zip(pieces, lows):
            for p in range(piece.shape[0] // SLAB):
                start = low + c * SLAB
                block = piece[p * SLAB : (p + 1) * SLAB, start : start + SLAB]
                turned = mm(swap, block.reshape(SLAB * SLAB, channels))
                turned_scr[c * SLAB : (c + 1) * SLAB, g * SLAB : (g + 1) * SLAB] = turned.astype(
                    BF16
                ).reshape(SLAB, SLAB, channels)
                g += 1

    def dense(i, carry):
        x = turned_scr[pl.ds(i * batch, batch)].reshape(batch * seqs, channels)
        normed = layer_normalize(x.astype(F32), gain_ref[...]).astype(BF16)
        q = (mm(normed, wqk_ref[:, :channels]) * scale).astype(BF16)
        q_scr[pl.ds(i * batch, batch)] = q.reshape(batch, seqs, channels)
        k = mm(normed, wqk_ref[:, channels:]).astype(BF16)
        k_scr[pl.ds(i * batch, batch)] = k.reshape(batch, seqs, channels)
        v = mm_nt(wvg_ref[:channels], normed).astype(BF16)
        gates = gate_of(mm_nt(wvg_ref[channels:], normed))
        for r in range(batch):
            v_scr[i * batch + r] = v[:, r * seqs : (r + 1) * seqs]
            gate_scr[i * batch + r] = gates[:, r * seqs : (r + 1) * seqs]
        return carry

    lax.fori_loop(0, local_res // batch, dense, 0)

    lane_head = lax.broadcasted_iota(jnp.int32, (seqs, channels), 1) // depth
    masked = jnp.broadcast_to(gap_ref[...] == 1, (seqs, halves * seqs))

    def attend(r, carry):
        q, k = q_scr[r], k_scr[r]
        q_block = jnp.concatenate(
            [jnp.where(lane_head // per == g, q, zero) for g in range(halves)], axis=0
        )
        weights = []
        for j in range(per):
            scores = mm_nt(jnp.where(lane_head % per == j, k, zero), q_block)
            weights.append(softmax_keys(jnp.where(masked, MASKED_SCORE, scores)))
        attended = [None] * heads
        blank = jnp.zeros((depth, seqs), BF16)
        for j in range(0, per, 2):
            left = []
            for jj in (j, j + 1):
                for g in range(halves):
                    h = g * per + jj
                    v = v_scr[r, h * depth : (h + 1) * depth]
                    left.append(jnp.concatenate([v, blank] if jj == j else [blank, v], axis=1))
            both = mm(
                jnp.concatenate(left, axis=0), jnp.concatenate(weights[j : j + 2], axis=0)
            )
            at = 0
            for jj in (j, j + 1):
                for g in range(halves):
                    attended[g * per + jj] = both[at : at + depth, g * seqs : (g + 1) * seqs]
                    at += depth
        gated = (jnp.concatenate(attended, axis=0) * gate_scr[r]).astype(BF16)
        gated_scr[r] = gated.T
        return carry

    lax.fori_loop(0, local_res, attend, 0)

    def finish(i, carry):
        x = turned_scr[pl.ds(i * batch, batch)].reshape(batch * seqs, channels)
        gated = gated_scr[pl.ds(i * batch, batch)].reshape(batch * seqs, channels)
        second = (x.astype(F32) + mm(gated, wout_ref[...])).astype(BF16)
        second_f = second.astype(F32)
        normed = layer_normalize(second_f, gain2_ref[...]).astype(BF16)
        hidden = jnp.maximum(mm(normed, widen_ref[...]), 0.0).astype(BF16)
        result = (second_f + mm(hidden, shrink_ref[...])).astype(BF16)
        done_scr[pl.ds(i * batch, batch)] = result.reshape(batch, seqs, channels)
        return carry

    lax.fori_loop(0, local_res // batch, finish, 0)
    if not turn:
        out_ref[...] = done_scr[...]
    base = 0
    for done_ref in done_refs:
        out_ref[:, base : base + done_ref.shape[1]] = done_ref[...]
        base += done_ref.shape[1]
    for c in range(slabs):
        for g in range(seqs // SLAB):
            block = done_scr[c * SLAB : (c + 1) * SLAB, g * SLAB : (g + 1) * SLAB]
            turned = mm(swap, block.reshape(SLAB * SLAB, channels))
            start = base + c * SLAB
            out_ref[g * SLAB : (g + 1) * SLAB, start : start + SLAB] = turned.astype(
                BF16
            ).reshape(SLAB, SLAB, channels)


def gather_bias(block, groups):
    if groups != 8:
        return lax.all_gather(block, "res", axis=0, tiled=False)
    side, lines = 2, groups // 2
    here = lax.axis_index("res")
    across = lax.ppermute(block, "res", [(i, i ^ 1) for i in range(groups)])
    odd = here % side == 1
    own = jnp.stack([jnp.where(odd, across, block), jnp.where(odd, block, across)])
    up, down = [own], [own]
    for _ in range(lines - 1):
        up.append(lax.ppermute(up[-1], "res", [(i, i + side) for i in range(groups - side)]))
        down.append(lax.ppermute(down[-1], "res", [(i, i - side) for i in range(side, groups)]))
    line = here // side
    pairs = []
    for at in range(lines):
        pairs.append(
            lax.select_n(line, *[up[z - at] if z >= at else down[at - z] for z in range(lines)])
        )
    return jnp.concatenate(pairs, axis=0)


def whole(count):
    return [pl.BlockSpec(memory_space=pltpu.VMEM)] * count


def body(
    aligned_chain_features,
    pair_representation_state,
    gap_block_flags,
    pair_norm_gain,
    pair_head_weight,
    horizontal_scaling_factor,
    row_input_weight,
    horizontal_final_matrix,
    vertical_scaling_factor,
    column_input_weight,
    vertical_final_matrix,
    feedforward_scaling_factor,
    feedforward_widen_matrix,
    feedforward_shrink_matrix,
):
    groups = lax.axis_size("res")
    total_seqs, local_res, channels = aligned_chain_features.shape
    residues = pair_representation_state.shape[1]
    heads = pair_head_weight.shape[1]
    local_seqs = total_seqs // groups
    turn = local_res % SLAB == 0
    seq_parts = 2 if turn and local_seqs % 2 == 0 else 1
    res_parts = local_res // SLAB if turn else 1
    part_seqs = local_seqs // seq_parts
    part_total = total_seqs // seq_parts
    part_res = local_res // res_parts
    here = lax.axis_index("res")

    def exchange(values):
        return lax.all_to_all(values, "res", split_axis=0, concat_axis=0, tiled=True)

    def kernel_call(kernel, name, micros, in_specs, out_shape, scratch):
        return pl.pallas_call(
            kernel,
            out_shape=jax.ShapeDtypeStruct(out_shape, BF16),
            in_specs=in_specs,
            out_specs=pl.BlockSpec(memory_space=pltpu.VMEM),
            scratch_shapes=scratch,
            compiler_params=pltpu.CompilerParams(vmem_limit_bytes=VMEM_BYTES),
            cost_estimate=pl.CostEstimate(
                flops=int(micros * 1e9), bytes_accessed=1 << 20, transcendentals=0
            ),
            name=name,
        )

    bias_local = kernel_call(
        bias_kernel, "pair_bias", 5, whole(3), (heads, local_res, residues),
        [pltpu.VMEM((local_res, heads, residues), F32)],
    )(pair_representation_state, pair_norm_gain[None, :], pair_head_weight.T)
    bias_all = gather_bias(bias_local, groups)
    row_qk, row_vg = row_input_weight[:, : 2 * channels], row_input_weight[:, 2 * channels :].T
    col_qk, col_vg = column_input_weight[:, : 2 * channels], column_input_weight[:, 2 * channels :].T

    def row_attention(part, arrived, low, count):
        gap = lax.dynamic_slice_in_dim(
            gap_block_flags, part * part_total + here * part_seqs, part_seqs, 0
        )
        return kernel_call(
            functools.partial(row_kernel, low, count), "row_attention",
            2 * part_seqs * count / local_res,
            [pl.BlockSpec(memory_space=pltpu.SMEM)] + whole(6),
            (groups, part_seqs, count, channels),
            [
                pltpu.VMEM((heads, residues, groups * count), F32),
                pltpu.VMEM((part_seqs, groups * count, channels), BF16),
                pltpu.VMEM((part_seqs, residues, channels), BF16),
                pltpu.VMEM((part_seqs, channels, residues), BF16),
                pltpu.VMEM((part_seqs, channels, groups * count), F32),
                pltpu.VMEM((part_seqs, groups * count, channels), BF16),
            ],
        )(
            gap, arrived, bias_all, horizontal_scaling_factor[None, :],
            row_qk, row_vg, horizontal_final_matrix,
        )

    arrived = [
        exchange(
            aligned_chain_features[p * part_total : (p + 1) * part_total].reshape(
                groups, part_seqs, local_res, channels
            )
        )
        for p in range(seq_parts)
    ]
    returned = []
    last = seq_parts - 1
    for p in range(last):
        first = row_attention(p, arrived[p], 0, local_res)
        first, arrived[p + 1] = lax.optimization_barrier((first, arrived[p + 1]))
        returned.append(exchange(first).reshape(part_total, local_res, channels))
    column_block = (here * local_res) // BLOCK
    col_gap = lax.dynamic_slice_in_dim(gap_block_flags, column_block, 1, 1)
    finals = []
    entries = arrived[last]
    for c in range(res_parts):
        first = row_attention(last, entries, c * part_res, part_res)
        first, entries = lax.optimization_barrier((first, entries))
        finals.append(exchange(first))
    done = []
    for c in range(res_parts):
        pieces = returned + [finals[c].reshape(part_total, part_res, channels)]
        if not turn:
            pieces = [jnp.swapaxes(piece, 0, 1) for piece in pieces]
        lows = (c * part_res,) * len(returned) + (0,)
        before = done if c == res_parts - 1 else []
        if not turn:
            shape = (part_res, total_seqs, channels)
        else:
            shape = (total_seqs, part_res * (1 + len(before)), channels)
        done.append(
            kernel_call(
                functools.partial(column_kernel, heads, turn, lows, len(before)),
                "column_transition", part_res, whole(len(pieces) + len(before) + 8), shape,
                [
                    pltpu.VMEM((part_res, total_seqs, channels), BF16),
                    pltpu.VMEM((part_res, total_seqs, channels), BF16),
                    pltpu.VMEM((part_res, total_seqs, channels), BF16),
                    pltpu.VMEM((part_res, channels, total_seqs), BF16),
                    pltpu.VMEM((part_res, channels, total_seqs), F32),
                    pltpu.VMEM((part_res, total_seqs, channels), BF16),
                    pltpu.VMEM((part_res, total_seqs, channels), BF16),
                ],
            )(
                *pieces, *before, col_gap, vertical_scaling_factor[None, :], col_qk, col_vg,
                vertical_final_matrix, feedforward_scaling_factor[None, :],
                feedforward_widen_matrix, feedforward_shrink_matrix,
            )
        )
    return done[-1] if turn else jnp.swapaxes(done[-1], 0, 1)


def solution(mesh):
    placed = (
        P("dp", "res", None),
        P(("dp", "res"), None, None),
        P("dp", None),
    ) + (P(),) * 11
    return jax.shard_map(
        body, mesh=mesh, in_specs=placed, out_specs=P("dp", "res", None), check_vma=False
    )
```

profile of v0, /device:TPU:0, one launch (start us, length us, event | category | flops | bytes accessed | tf_op | source)
XLA Modules:
  0.0 208.7 jit_solution(6125696922394435770)
XLA Ops:
  0.0 3.1 %fusion = (bf16[64,32,256]{2,1,0:T(8,128)(2,1)}, bf16[64,32,256]{2,1,0:T(8,128)(2,1)}) fusion(bf16[128,32,256]{2,1,0:T(8,128)(2,1)} %param.14), kind=kLoop, calls=%fused_computation.11 | loop fusion | bytes 4194304 | tf_op jit(solution)/shard_map/slice | solution.py:369
  3.1 7.4 %all-to-all-start = ((bf16[8,8,32,256]{3,2,1,0:T(8,128)(2,1)}), bf16[8,8,32,256]{3,2,1,0:T(8,128)(2,1)S(1)}, u32[]{:S(2)}, u32[]{:S(2)}) async-start(bf16[8,8,32,256]{3,2,1,0:T(8,128)(2,1)} %bitcast.34), calls=%async_computation | async-start | bytes 2097152 | tf_op jit(solution)/shard_map/all_to_all | solution.py:321
  10.5 4.0 %pair_bias.1 = bf16[8,32,256]{2,1,0:T(8,128)(2,1)S(1)} custom-call(bf16[32,256,128]{2,1,0:T(8,128)(2,1)S(1)} %copy-done.10, f32[1,128]{1,0:T(1,128)S(1)} %bitcast.33, bf16[8,128]{1,0:T(8,128)(2,1)S(1)} %bitcast.25), custom_call_target="tpu_custom_call" | custom-call | flops 5000000000 | bytes 1048576 | tf_op jit(solution)/shard_map/pair_bias/pallas_call | solution.py:337
  14.5 2.1 collective-permute-start
  16.6 7.1 %collective-permute-done = bf16[8,32,256]{2,1,0:T(8,128)(2,1)S(1)} collective-permute-done((bf16[8,32,256]{2,1,0:T(8,128)(2,1)S(1)}, bf16[8,32,256]{2,1,0:T(8,128)(2,1)S(1)}, u32[]{:S(2)}, u32[]{:S(2)}) %collective-permute-start) | collective-permute-done | bytes 131104 | tf_op jit(solution)/shard_map/ppermute | solution.py:271
  23.7 1.9 collective-permute-start.1
  25.6 1.3 collective-permute-start.4
  26.9 6.3 %collective-permute-done.1 = bf16[2,8,32,256]{3,2,1,0:T(8,128)(2,1)S(1)} collective-permute-done((bf16[2,8,32,256]{3,2,1,0:T(8,128)(2,1)S(1)}, bf16[2,8,32,256]{3,2,1,0:T(8,128)(2,1)S(1)}, u32[]{:S(2)}, u32[]{:S(2)}) %collective-permute-start.1) | collective-permute-done | bytes 262176 | tf_op jit(solution)/shard_map/ppermute | solution.py:276
  33.2 9.7 %collective-permute-start.2 = (bf16[2,8,32,256]{3,2,1,0:T(8,128)(2,1)S(1)}, bf16[2,8,32,256]{3,2,1,0:T(8,128)(2,1)}, u32[]{:S(2)}, u32[]{:S(2)}) collective-permute-start(bf16[2,8,32,256]{3,2,1,0:T(8,128)(2,1)S(1)} %collective-permute-done.1), channel_id=1, source_target_pairs={{0,8},{4,12},{8,16},{12,20},{16,24},{20,28},{1,9},{5,13},{9,17},{1... | collective-permute-start | bytes 786440 | tf_op jit(solution)/shard_map/ppermute | solution.py:276
  42.8 1.3 collective-permute-start.5
  44.1 3.7 %collective-permute-done.2 = bf16[2,8,32,256]{3,2,1,0:T(8,128)(2,1)} collective-permute-done((bf16[2,8,32,256]{3,2,1,0:T(8,128)(2,1)S(1)}, bf16[2,8,32,256]{3,2,1,0:T(8,128)(2,1)}, u32[]{:S(2)}, u32[]{:S(2)}) %collective-permute-start.2) | collective-permute-done | bytes 262176 | tf_op jit(solution)/shard_map/ppermute | solution.py:276
  47.9 5.2 %collective-permute-start.3 = (bf16[2,8,32,256]{3,2,1,0:T(8,128)(2,1)}, bf16[2,8,32,256]{3,2,1,0:T(8,128)(2,1)}, u32[]{:S(2)}, u32[]{:S(2)}) collective-permute-start(bf16[2,8,32,256]{3,2,1,0:T(8,128)(2,1)} %collective-permute-done.2), channel_id=1, source_target_pairs={{0,8},{4,12},{8,16},{12,20},{16,24},{20,28},{1,9},{5,13},{9,17},{1... | collective-permute-start | bytes 786440 | tf_op jit(solution)/shard_map/ppermute | solution.py:276
  53.1 1.3 collective-permute-start.6
  54.6 1.8 fusion.2
  56.6 6.7 %all-to-all-start.1 = ((bf16[8,8,32,256]{3,2,1,0:T(8,128)(2,1)}), bf16[8,8,32,256]{3,2,1,0:T(8,128)(2,1)S(1)}, u32[]{:S(2)}, u32[]{:S(2)}) async-start(bf16[8,8,32,256]{3,2,1,0:T(8,128)(2,1)} %bitcast.7), calls=%async_computation.1 | async-start | bytes 2097152 | tf_op jit(solution)/shard_map/all_to_all | solution.py:321
  63.4 1.3 select_select_fusion.3
  64.8 22.0 %row_attention.3 = bf16[8,8,32,256]{3,2,1,0:T(8,128)(2,1)S(1)} custom-call(s32[8,2]{1,0:T(8,128)S(1)} %copy.20.gap_ref, bf16[8,8,32,256]{3,2,1,0:T(8,128)(2,1)S(1)} %all-to-all-done.x_ref, bf16[8,8,32,256]{3,2,1,0:T(8,128)(2,1)S(1)} %pad_maximum_fusion.bias_ref, f32[1,256]{1,0:T(1,128)S(1)} %bitcast.26, bf16[256,512]{1,0:T(8,128)(2,1)S(1)} %copy-done.5, ...), custom_call_target="tpu_custom_call" | custom-call | flops 16000000000 | bytes 1048576 | tf_op jit(solution)/shard_map/row_attention/pallas_call | solution.py:349
  86.9 1.0 copy-done
  90.2 18.7 %row_attention.4 = bf16[8,8,16,256]{3,2,1,0:T(8,128)(2,1)S(1)} custom-call(s32[8,2]{1,0:T(8,128)S(1)} %copy.22.gap_ref, bf16[8,8,32,256]{3,2,1,0:T(8,128)(2,1)S(1)} %all-to-all-done.1.x_ref, bf16[8,8,32,256]{3,2,1,0:T(8,128)(2,1)S(1)} %pad_maximum_fusion.bias_ref, f32[1,256]{1,0:T(1,128)S(1)} %bitcast.27, bf16[256,512]{1,0:T(8,128)(2,1)S(1)} %copy-done.6, ...), custom_call_target="tpu_custom_call" | custom-call | flops 8000000000 | bytes 1048576 | tf_op jit(solution)/shard_map/row_attention/pallas_call | solution.py:349
  108.9 18.4 %all_to_all.25 = bf16[8,8,16,256]{3,2,1,0:T(8,128)(2,1)} all-to-all(bf16[8,8,16,256]{3,2,1,0:T(8,128)(2,1)S(1)} %row_attention.4), channel_id=1, replica_groups=mesh['res'=8,'dp'=4] {'res'}, dimensions={0} | all-to-all | bytes 1048576 | tf_op jit(solution)/shard_map/all_to_all | solution.py:321
  127.3 3.6 %all-to-all-start.2 = ((bf16[8,8,32,256]{3,2,1,0:T(8,128)(2,1)}), bf16[8,8,32,256]{3,2,1,0:T(8,128)(2,1)S(1)}, u32[]{:S(2)}, u32[]{:S(2)}) async-start(bf16[8,8,32,256]{3,2,1,0:T(8,128)(2,1)} %copy-done), calls=%async_computation.2 | async-start | bytes 2097152 | tf_op jit(solution)/shard_map/all_to_all | solution.py:321
  131.1 1.9 fusion.1
  132.9 1.8 copy.24
  136.6 18.8 %row_attention.5 = bf16[8,8,16,256]{3,2,1,0:T(8,128)(2,1)S(1)} custom-call(s32[8,2]{1,0:T(8,128)S(1)} %copy.22.gap_ref, bf16[8,8,32,256]{3,2,1,0:T(8,128)(2,1)S(1)} %all-to-all-done.1.x_ref, bf16[8,8,32,256]{3,2,1,0:T(8,128)(2,1)S(1)} %pad_maximum_fusion.bias_ref, f32[1,256]{1,0:T(1,128)S(1)} %bitcast.28, bf16[256,512]{1,0:T(8,128)(2,1)S(1)} %copy-done.7, ...), custom_call_target="tpu_custom_call" | custom-call | flops 8000000000 | bytes 1048576 | tf_op jit(solution)/shard_map/row_attention/pallas_call | solution.py:349
  156.4 5.8 %all-to-all-start.3 = ((bf16[8,8,16,256]{3,2,1,0:T(8,128)(2,1)}), bf16[8,8,16,256]{3,2,1,0:T(8,128)(2,1)S(1)}, u32[]{:S(2)}, u32[]{:S(2)}) async-start(bf16[8,8,16,256]{3,2,1,0:T(8,128)(2,1)} %copy-done.2), calls=%async_computation.3 | async-start | bytes 1048576 | tf_op jit(solution)/shard_map/all_to_all | solution.py:321
  162.2 1.0 copy-done.1
  165.2 1.0 copy-done.11
  166.2 1.0 copy-done.13
  168.2 18.5 %column_transition.2.refs_2_ = bf16[128,16,256]{2,1,0:T(8,128)(2,1)S(1)} custom-call(bf16[64,32,256]{2,1,0:T(8,128)(2,1)S(1)} %bitcast.16, bf16[64,16,256]{2,1,0:T(8,128)(2,1)S(1)} %bitcast.18, s32[128,1]{1,0:T(8,128)S(1)} %copy.23.refs_2_.refs_3_, f32[1,256]{1,0:T(1,128)S(1)} %bitcast.29, bf16[256,512]{1,0:T(8,128)(2,1)S(1)} %copy-done.8, ...), custom_call_target="tpu_custom_call" | custom-call | flops 16000000000 | bytes 1048576 | tf_op jit(solution)/shard_map/column_transition/pallas_call | solution.py:401
  186.7 1.0 copy-done.25
  187.7 1.2 copy-done.26
  188.9 19.8 %column_transition.3 = bf16[128,32,256]{2,1,0:T(8,128)(2,1)} custom-call(bf16[64,32,256]{2,1,0:T(8,128)(2,1)S(1)} %bitcast.17, bf16[64,16,256]{2,1,0:T(8,128)(2,1)S(1)} %bitcast.19, bf16[128,16,256]{2,1,0:T(8,128)(2,1)S(1)} %copy-done.26, s32[128,1]{1,0:T(8,128)S(1)} %copy.23.refs_2_.refs_3_, f32[1,256]{1,0:T(1,128)S(1)} %bitcast.30, ...), custom_call_target="tpu_custom_call" | custom-call | flops 16000000000 | bytes 1048576 | tf_op jit(solution)/shard_map/column_transition/pallas_call | solution.py:401
  (67 shorter events, 8.8 us)
Async XLA Ops:
  3.1 7.4 %copy-start.10 = (bf16[32,256,128]{2,1,0:T(8,128)(2,1)S(1)}, bf16[32,256,128]{2,1,0:T(8,128)(2,1)}, u32[]{:S(2)}) copy-start(bf16[32,256,128]{2,1,0:T(8,128)(2,1)} %pair_ref.1) | copy-start | bytes 6291460
  3.1 7.4 %copy-start.20 = (bf16[128,8]{0,1:T(8,128)(2,1)S(1)}, bf16[128,8]{0,1:T(8,128)(2,1)}, u32[]{:S(2)}) copy-start(bf16[128,8]{0,1:T(8,128)(2,1)} %param.18) | copy-start | bytes 6148
  3.1 7.4 %copy-start.24 = (f32[128]{0:T(128)S(1)}, f32[128]{0:T(128)}, u32[]{:S(2)}) copy-start(f32[128]{0:T(128)} %param.17) | copy-start | bytes 1540
  3.1 53.5 %all-to-all-start = ((bf16[8,8,32,256]{3,2,1,0:T(8,128)(2,1)}), bf16[8,8,32,256]{3,2,1,0:T(8,128)(2,1)S(1)}, u32[]{:S(2)}, u32[]{:S(2)}) async-start(bf16[8,8,32,256]{3,2,1,0:T(8,128)(2,1)} %bitcast.34), calls=%async_computation | async-start | bytes 2097152 | tf_op jit(solution)/shard_map/all_to_all | solution.py:321
  10.5 43.9 %copy-start.27 = (s32[128,2]{0,1:T(2,128)S(1)}, s32[128,2]{0,1:T(2,128)}, u32[]{:S(2)}) copy-start(s32[128,2]{0,1:T(2,128)} %param.16) | copy-start | bytes 3076
  14.5 9.1 %collective-permute-start = (bf16[8,32,256]{2,1,0:T(8,128)(2,1)S(1)}, bf16[8,32,256]{2,1,0:T(8,128)(2,1)S(1)}, u32[]{:S(2)}, u32[]{:S(2)}) collective-permute-start(bf16[8,32,256]{2,1,0:T(8,128)(2,1)S(1)} %pair_bias.1), channel_id=1, source_target_pairs={{0,4},{4,0},{8,12},{12,8},{16,20},{20,16},{24,28},{28,24},{1,5},{5... | collective-permute-start | bytes 393224 | tf_op jit(solution)/shard_map/ppermute | solution.py:271
  23.7 9.5 %collective-permute-start.1 = (bf16[2,8,32,256]{3,2,1,0:T(8,128)(2,1)S(1)}, bf16[2,8,32,256]{3,2,1,0:T(8,128)(2,1)S(1)}, u32[]{:S(2)}, u32[]{:S(2)}) collective-permute-start(bf16[2,8,32,256]{3,2,1,0:T(8,128)(2,1)S(1)} %pad_maximum_fusion.1), channel_id=1, source_target_pairs={{0,8},{4,12},{8,16},{12,20},{16,24},{20,28},{1,9},{5,13},{9,17},{1... | collective-permute-start | bytes 786440 | tf_op jit(solution)/shard_map/ppermute | solution.py:276
  25.6 17.2 %collective-permute-start.4 = (bf16[2,8,32,256]{3,2,1,0:T(8,128)(2,1)S(1)}, bf16[2,8,32,256]{3,2,1,0:T(8,128)(2,1)S(1)}, u32[]{:S(2)}, u32[]{:S(2)}) collective-permute-start(bf16[2,8,32,256]{3,2,1,0:T(8,128)(2,1)S(1)} %pad_maximum_fusion.1), channel_id=1, source_target_pairs={{8,0},{12,4},{16,8},{20,12},{24,16},{28,20},{9,1},{13,5},{17,9},{2... | collective-permute-start | bytes 786440 | tf_op jit(solution)/shard_map/ppermute | solution.py:277
  33.2 14.7 %collective-permute-start.2 = (bf16[2,8,32,256]{3,2,1,0:T(8,128)(2,1)S(1)}, bf16[2,8,32,256]{3,2,1,0:T(8,128)(2,1)}, u32[]{:S(2)}, u32[]{:S(2)}) collective-permute-start(bf16[2,8,32,256]{3,2,1,0:T(8,128)(2,1)S(1)} %collective-permute-done.1), channel_id=1, source_target_pairs={{0,8},{4,12},{8,16},{12,20},{16,24},{20,28},{1,9},{5,13},{9,17},{1... | collective-permute-start | bytes 786440 | tf_op jit(solution)/shard_map/ppermute | solution.py:276
  42.8 10.3 %collective-permute-start.5 = (bf16[2,8,32,256]{3,2,1,0:T(8,128)(2,1)S(1)}, bf16[2,8,32,256]{3,2,1,0:T(8,128)(2,1)}, u32[]{:S(2)}, u32[]{:S(2)}) collective-permute-start(bf16[2,8,32,256]{3,2,1,0:T(8,128)(2,1)S(1)} %collective-permute-done.4), channel_id=1, source_target_pairs={{8,0},{12,4},{16,8},{20,12},{24,16},{28,20},{9,1},{13,5},{17,9},{2... | collective-permute-start | bytes 786440 | tf_op jit(solution)/shard_map/ppermute | solution.py:277
  47.9 15.5 %collective-permute-start.3 = (bf16[2,8,32,256]{3,2,1,0:T(8,128)(2,1)}, bf16[2,8,32,256]{3,2,1,0:T(8,128)(2,1)}, u32[]{:S(2)}, u32[]{:S(2)}) collective-permute-start(bf16[2,8,32,256]{3,2,1,0:T(8,128)(2,1)} %collective-permute-done.2), channel_id=1, source_target_pairs={{0,8},{4,12},{8,16},{12,20},{16,24},{20,28},{1,9},{5,13},{9,17},{1... | collective-permute-start | bytes 786440 | tf_op jit(solution)/shard_map/ppermute | solution.py:276
  53.1 10.2 %collective-permute-start.6 = (bf16[2,8,32,256]{3,2,1,0:T(8,128)(2,1)}, bf16[2,8,32,256]{3,2,1,0:T(8,128)(2,1)}, u32[]{:S(2)}, u32[]{:S(2)}) collective-permute-start(bf16[2,8,32,256]{3,2,1,0:T(8,128)(2,1)} %collective-permute-done.5), channel_id=1, source_target_pairs={{8,0},{12,4},{16,8},{20,12},{24,16},{28,20},{9,1},{13,5},{17,9},{2... | collective-permute-start | bytes 786440 | tf_op jit(solution)/shard_map/ppermute | solution.py:277
  56.6 31.8 %all-to-all-start.1 = ((bf16[8,8,32,256]{3,2,1,0:T(8,128)(2,1)}), bf16[8,8,32,256]{3,2,1,0:T(8,128)(2,1)S(1)}, u32[]{:S(2)}, u32[]{:S(2)}) async-start(bf16[8,8,32,256]{3,2,1,0:T(8,128)(2,1)} %bitcast.7), calls=%async_computation.1 | async-start | bytes 2097152 | tf_op jit(solution)/shard_map/all_to_all | solution.py:321
  63.3 1.5 copy-start.5
  63.3 1.5 copy-start.15
  63.3 1.5 copy-start.21
  86.8 1.0 copy-start
  88.4 1.0 copy-start.6
  127.3 29.1 %all-to-all-start.2 = ((bf16[8,8,32,256]{3,2,1,0:T(8,128)(2,1)}), bf16[8,8,32,256]{3,2,1,0:T(8,128)(2,1)S(1)}, u32[]{:S(2)}, u32[]{:S(2)}) async-start(bf16[8,8,32,256]{3,2,1,0:T(8,128)(2,1)} %copy-done), calls=%async_computation.2 | async-start | bytes 2097152 | tf_op jit(solution)/shard_map/all_to_all | solution.py:321
  136.6 25.6 %copy-start.22 = (f32[256]{0:T(256)S(1)}, f32[256]{0:T(256)}, u32[]{:S(2)}) copy-start(f32[256]{0:T(256)} %param.22) | copy-start | bytes 3076
  136.6 25.6 %copy-start.23 = (f32[256]{0:T(256)S(1)}, f32[256]{0:T(256)}, u32[]{:S(2)}) copy-start(f32[256]{0:T(256)} %param.25) | copy-start | bytes 3076
  156.4 31.3 %all-to-all-start.3 = ((bf16[8,8,16,256]{3,2,1,0:T(8,128)(2,1)}), bf16[8,8,16,256]{3,2,1,0:T(8,128)(2,1)S(1)}, u32[]{:S(2)}, u32[]{:S(2)}) async-start(bf16[8,8,16,256]{3,2,1,0:T(8,128)(2,1)} %copy-done.2), calls=%async_computation.3 | async-start | bytes 1048576 | tf_op jit(solution)/shard_map/all_to_all | solution.py:321
  162.2 1.0 copy-start.1
  165.2 1.0 copy-start.11
  166.2 1.0 copy-start.13
  168.1 19.5 %copy-start.4 = (bf16[256,512]{0,1:T(8,128)(2,1)S(1)}, bf16[256,512]{0,1:T(8,128)(2,1)}, u32[]{:S(2)}) copy-start(bf16[256,512]{0,1:T(8,128)(2,1)} %copy.24) | copy-start | bytes 786436
  168.1 19.5 %copy-start.9 = (bf16[256,512]{1,0:T(8,128)(2,1)S(1)}, bf16[256,512]{1,0:T(8,128)(2,1)}, u32[]{:S(2)}) copy-start(bf16[256,512]{1,0:T(8,128)(2,1)} %get-tuple-element.22.refs_4_.refs_5_) | copy-start | bytes 786436
  168.2 19.5 %copy-start.12 = (bf16[256,1024]{1,0:T(8,128)(2,1)S(1)}, bf16[256,1024]{1,0:T(8,128)(2,1)}, u32[]{:S(2)}) copy-start(bf16[256,1024]{1,0:T(8,128)(2,1)} %refs_9_.3) | copy-start | bytes 1572868
  168.2 19.5 %copy-start.14 = (bf16[1024,256]{1,0:T(8,128)(2,1)S(1)}, bf16[1024,256]{1,0:T(8,128)(2,1)}, u32[]{:S(2)}) copy-start(bf16[1024,256]{1,0:T(8,128)(2,1)} %refs_10_.1) | copy-start | bytes 1572868
  168.2 19.5 %copy-start.19 = (bf16[256,256]{1,0:T(8,128)(2,1)S(1)}, bf16[256,256]{1,0:T(8,128)(2,1)}, u32[]{:S(2)}) copy-start(bf16[256,256]{1,0:T(8,128)(2,1)} %refs_7_.1) | copy-start | bytes 393220
  186.7 1.0 copy-start.25
  187.7 1.2 copy-start.26
  (7 other events, 6.4 us)
where the time goes:
time: 210 us; the launch traced here: 209 us
  Pallas kernels  102 us (49%)
  starting transfers between devices  46.3 us (22%)
  local copies, waits for them, and re-layouts  22.7 us (11%)
  blocking collectives  18.4 us (9%)
  waiting for transfers between devices  17.8 us (8%)
    pallas_call x3, Pallas kernels, row_attention(): kernel_call(functools.partial(row_kernel, low, count), 'row_attention', 2...  59.5 us
    pallas_call x2, Pallas kernels, body(): kernel_call(functools.partial(column_kernel, heads, turn, lows, len(befor...  38.3 us
    all_to_all x4, starting transfers between devices, exchange(): lax.all_to_all(values, 'res', split_axis=0, concat_axis=0, tiled=True)  23.6 us
    all_to_all x1, blocking collectives, exchange(): lax.all_to_all(values, 'res', split_axis=0, concat_axis=0, tiled=True)  18.4 us
    ppermute x3, starting transfers between devices, gather_bias(): lax.ppermute(up[-1], 'res', [(i, i + side) for i in range(groups - side)])  16.8 us
    unnamed x61, local copies, waits for them, and re-layouts  15.9 us
    ppermute x3, waiting for transfers between devices, gather_bias(): lax.ppermute(up[-1], 'res', [(i, i + side) for i in range(groups - side)])  10 us
    ppermute x1, waiting for transfers between devices, gather_bias(): across = lax.ppermute(block, 'res', [(i, i ^ 1) for i in range(groups)])  7.06 us
  transfers between devices with their start and end apart: 11, of which 5 were waited for; matrix products, arithmetic and copies ran while one was open for 4% of the time, Pallas kernels for 30%

commit v1 on v0

v1 whole, which is shorter than its diff:
```python
import functools

import jax
import jax.numpy as jnp
from jax import lax
from jax.experimental import pallas as pl
from jax.experimental.pallas import tpu as pltpu
from jax.sharding import PartitionSpec as P

BLOCK = 128
EPSILON = 1e-05
MASKED_SCORE = -1000000000.0
LANES = 128
SLAB = 16
F32 = jnp.float32
BF16 = jnp.bfloat16
VMEM_BYTES = 48 * 1024 * 1024


def layer_normalize(values_f, scale_gain):
    centred = values_f - jnp.mean(values_f, axis=-1, keepdims=True)
    spread = jnp.mean(centred * centred, axis=-1, keepdims=True)
    return centred * lax.rsqrt(spread + EPSILON) * scale_gain


def mm(lhs, rhs):
    return jnp.dot(lhs, rhs, preferred_element_type=F32)


def mm_nt(lhs, rhs):
    return lax.dot_general(lhs, rhs, (((1,), (1,)), ((), ())), preferred_element_type=F32)


def swap_matrix(outer, inner):
    size = outer * inner
    to = lax.broadcasted_iota(jnp.int32, (size, size), 0)
    come = lax.broadcasted_iota(jnp.int32, (size, size), 1)
    source = lax.rem(to, outer) * inner + lax.div(to, outer)
    return jnp.where(come == source, 1.0, 0.0).astype(BF16)


def bias_kernel(pair_ref, gain_ref, weight_ref, out_ref, rows_scr):
    heads, local_res, residues = out_ref.shape
    channels = pair_ref.shape[2]
    step = min(4, local_res)

    def body(i, carry):
        block = pair_ref[pl.ds(i * step, step)].reshape(step * residues, channels)
        normed = layer_normalize(block.astype(F32), gain_ref[...]).astype(BF16)
        projected = mm_nt(weight_ref[...], normed)
        for j in range(step):
            rows_scr[i * step + j] = projected[:, j * residues : (j + 1) * residues]
        return carry

    lax.fori_loop(0, local_res // step, body, 0)
    rows = rows_scr[...].reshape(local_res * heads, residues).astype(BF16)
    turned = mm(swap_matrix(local_res, heads), rows)
    out_ref[...] = turned.reshape(heads, local_res, residues).astype(BF16)


def softmax_keys(scores):
    e = jnp.exp(scores - jnp.max(scores, axis=0, keepdims=True))
    return (e * (1.0 / jnp.sum(e, axis=0, keepdims=True))).astype(BF16)


def gate_of(values):
    return 0.5 * jnp.tanh(0.5 * values) + 0.5


def stack(parts, axis):
    return parts[0] if len(parts) == 1 else jnp.concatenate(parts, axis=axis)


def softmax_keys(scores):
    e = jnp.exp(scores - jnp.max(scores, axis=0, keepdims=True))
    return (e * (1.0 / jnp.sum(e, axis=0, keepdims=True))).astype(BF16)


def gate_of(values):
    return 0.5 * jnp.tanh(0.5 * values) + 0.5


def stack(parts, axis):
    return parts[0] if len(parts) == 1 else jnp.concatenate(parts, axis=axis)


def head_blocks(q, depth):
    heads = q.shape[0] // depth
    zero = jnp.zeros((depth, q.shape[1]), BF16)
    columns = []
    for h in range(heads):
        blocks = [q[h * depth : (h + 1) * depth] if i == h else zero for i in range(heads)]
        columns.append(jnp.concatenate(blocks, axis=0))
    return jnp.concatenate(columns, axis=1)


def start_copies(sources, targets, sems):
    copies = [
        pltpu.make_async_copy(source, target, sems.at[i])
        for i, (source, target) in enumerate(zip(sources, targets))
    ]
    for copy in copies:
        copy.start()
    return copies


def row_kernel(
    low, count, gap_ref, gain_ref, x_hbm, wk_hbm, wv_hbm, wqg_hbm, wout_hbm, bias_hbm, out_ref,
    x_ref, wk_ref, wv_ref, wqg_ref, wout_ref, bias_ref, sems,
    bias_scr, q_scr, k_scr, v_scr, gate_scr, gated_scr,
):
    copies = start_copies(
        [x_hbm, wk_hbm, wv_hbm, wqg_hbm, wout_hbm, bias_hbm],
        [x_ref, wk_ref, wv_ref, wqg_ref, wout_ref, bias_ref],
        sems,
    )
    groups, seqs, local_res, channels = x_ref.shape
    heads = bias_ref.shape[1]
    residues = groups * local_res
    queries = groups * count
    depth = channels // heads
    per = LANES // depth
    scale = depth ** (-0.5)
    pair = 2 if seqs % 2 == 0 else 1
    for copy in copies[:4]:
        copy.wait()

    def dense(i, carry):
        normed, mine = [], []
        for j in range(pair):
            x = x_ref[:, pl.ds(i * pair + j, 1)].reshape(residues, channels)
            n = layer_normalize(x.astype(F32), gain_ref[...]).astype(BF16)
            normed.append(n)
            if count != local_res:
                n = n.reshape(groups, local_res, channels)[:, low : low + count]
                n = n.reshape(queries, channels)
            mine.append(n)
        normed, mine = stack(normed, 0), stack(mine, 0)
        k = mm(normed, wk_ref[...]).astype(BF16)
        v = mm(wv_ref[...], normed.T).astype(BF16)
        qg = mm(wqg_ref[...], mine.T)
        q = (qg[:channels] * scale).astype(BF16)
        gates = gate_of(qg[channels:])
        for j in range(pair):
            s = i * pair + j
            q_scr[s] = q[:, j * queries : (j + 1) * queries]
            k_scr[s] = k[j * residues : (j + 1) * residues]
            v_scr[s] = v[:, j * residues : (j + 1) * residues]
            gate_scr[s] = gates[:, j * queries : (j + 1) * queries]
        return carry

    lax.fori_loop(0, seqs // pair, dense, 0)

    copies[5].wait()
    for h in range(heads):
        block = bias_ref[:, h, low : low + count].reshape(queries, residues)
        bias_scr[h] = block.T.astype(F32)
    bias_scr[heads] = jnp.full((residues, queries), MASKED_SCORE, F32)

    def attend(s, carry):
        gaps = [gap_ref[s, b] == 1 for b in range(residues // BLOCK)]
        attended = [None] * heads
        for g in range(heads // per):
            lanes = slice(g * LANES, (g + 1) * LANES)
            scores = mm(k_scr[s, :, lanes], head_blocks(q_scr[s, lanes], depth))
            weights = []
            for j in range(per):
                h = g * per + j
                bias = [
                    bias_scr[jnp.where(gap, heads, h), b * BLOCK : (b + 1) * BLOCK]
                    for b, gap in enumerate(gaps)
                ]
                own = scores[:, j * queries : (j + 1) * queries]
                weights.append(softmax_keys(own + stack(bias, 0)))
            for j in range(0, per, 2):
                h = g * per + j
                both = mm(
                    v_scr[s, h * depth : (h + 2) * depth],
                    jnp.concatenate(weights[j : j + 2], axis=1),
                )
                attended[h] = both[:depth, :queries]
                attended[h + 1] = both[depth:, queries:]
        gated = (jnp.concatenate(attended, axis=0) * gate_scr[s]).astype(BF16)
        gated_scr[s] = gated.T
        return carry

    lax.fori_loop(0, seqs, attend, 0)
    copies[4].wait()

    def finish(i, carry):
        gated = gated_scr[pl.ds(i * pair, pair)].reshape(pair * queries, channels)
        update = mm(gated, wout_ref[...])
        for j in range(pair):
            s = i * pair + j
            x = x_ref[:, pl.ds(s, 1), low : low + count].reshape(queries, channels)
            result = x.astype(F32) + update[j * queries : (j + 1) * queries]
            out_ref[:, pl.ds(s, 1)] = result.astype(BF16).reshape(groups, 1, count, channels)
        return carry

    lax.fori_loop(0, seqs // pair, finish, 0)


def column_kernel(
    heads, turn, earlier, gap_ref, gain_ref, gain2_ref, x_hbm, wk_hbm, wqvg_hbm, wout_hbm,
    widen_hbm, shrink_hbm, *refs,
):
    done_refs, refs = refs[:earlier], refs[earlier:]
    (out_ref, x_ref, wk_ref, wqvg_ref, wout_ref, widen_ref, shrink_ref, sems) = refs[:8]
    (turned_scr, q_scr, k_scr, v_scr, gate_scr, gated_scr, done_scr) = refs[8:]
    copies = start_copies(
        [x_hbm, wk_hbm, wqvg_hbm, wout_hbm, widen_hbm, shrink_hbm],
        [x_ref, wk_ref, wqvg_ref, wout_ref, widen_ref, shrink_ref],
        sems,
    )
    local_res, seqs, channels = turned_scr.shape
    depth = channels // heads
    per = LANES // depth
    scale = depth ** (-0.5)
    batch = min(4, local_res)
    slabs = local_res // SLAB if turn else 0
    swap = swap_matrix(SLAB, SLAB)
    base = 0
    for done_ref in done_refs:
        out_ref[:, base : base + done_ref.shape[1]] = done_ref[...]
        base += done_ref.shape[1]
    copies[0].wait()
    if not turn:
        turned_scr[...] = x_ref[...]
    for c in range(slabs):
        for g in range(seqs // SLAB):
            block = x_ref[g * SLAB : (g + 1) * SLAB, c * SLAB : (c + 1) * SLAB]
            turned = mm(swap, block.reshape(SLAB * SLAB, channels))
            turned_scr[c * SLAB : (c + 1) * SLAB, g * SLAB : (g + 1) * SLAB] = turned.astype(
                BF16
            ).reshape(SLAB, SLAB, channels)
    for copy in copies[1:3]:
        copy.wait()

    def dense(i, carry):
        x = turned_scr[pl.ds(i * batch, batch)].reshape(batch * seqs, channels)
        normed = layer_normalize(x.astype(F32), gain_ref[...]).astype(BF16)
        k = mm(normed, wk_ref[...]).astype(BF16)
        k_scr[pl.ds(i * batch, batch)] = k.reshape(batch, seqs, channels)
        qvg = mm(wqvg_ref[...], normed.T)
        q = (qvg[:channels] * scale).astype(BF16)
        v = qvg[channels : 2 * channels].astype(BF16)
        gates = gate_of(qvg[2 * channels :])
        for r in range(batch):
            q_scr[i * batch + r] = q[:, r * seqs : (r + 1) * seqs]
            v_scr[i * batch + r] = v[:, r * seqs : (r + 1) * seqs]
            gate_scr[i * batch + r] = gates[:, r * seqs : (r + 1) * seqs]
        return carry

    lax.fori_loop(0, local_res // batch, dense, 0)

    mask = jnp.broadcast_to(jnp.where(gap_ref[...] == 1, MASKED_SCORE, 0.0), (seqs, seqs))

    def attend(r, carry):
        attended = [None] * heads
        blank = jnp.zeros((2 * depth, seqs), BF16)
        for g in range(heads // per):
            lanes = slice(g * LANES, (g + 1) * LANES)
            scores = mm(k_scr[r, :, lanes], head_blocks(q_scr[r, lanes], depth))
            weights = [
                softmax_keys(scores[:, j * seqs : (j + 1) * seqs] + mask) for j in range(per)
            ]
            for j in range(0, per, 4):
                h = g * per + j
                v = v_scr[r, h * depth : (h + 4) * depth]
                left = jnp.concatenate(
                    [
                        jnp.concatenate([v[: 2 * depth], blank], axis=1),
                        jnp.concatenate([blank, v[2 * depth :]], axis=1),
                    ],
                    axis=0,
                )
                right = jnp.concatenate(
                    [
                        jnp.concatenate(weights[j : j + 2], axis=1),
                        jnp.concatenate(weights[j + 2 : j + 4], axis=1),
                    ],
                    axis=0,
                )
                both = mm(left, right)
                for e in range(4):
                    at = (e % 2) * seqs
                    attended[h + e] = both[e * depth : (e + 1) * depth, at : at + seqs]
        gated = (jnp.concatenate(attended, axis=0) * gate_scr[r]).astype(BF16)
        gated_scr[r] = gated.T
        return carry

    lax.fori_loop(0, local_res, attend, 0)
    for copy in copies[3:]:
        copy.wait()

    def finish(i, carry):
        x = turned_scr[pl.ds(i * batch, batch)].reshape(batch * seqs, channels)
        gated = gated_scr[pl.ds(i * batch, batch)].reshape(batch * seqs, channels)
        second = (x.astype(F32) + mm(gated, wout_ref[...])).astype(BF16)
        second_f = second.astype(F32)
        normed = layer_normalize(second_f, gain2_ref[...]).astype(BF16)
        hidden = jnp.maximum(mm(normed, widen_ref[...]), 0.0).astype(BF16)
        result = (second_f + mm(hidden, shrink_ref[...])).astype(BF16)
        done_scr[pl.ds(i * batch, batch)] = result.reshape(batch, seqs, channels)
        return carry

    lax.fori_loop(0, local_res // batch, finish, 0)
    if not turn:
        out_ref[...] = done_scr[...]
    for c in range(slabs):
        for g in range(seqs // SLAB):
            block = done_scr[c * SLAB : (c + 1) * SLAB, g * SLAB : (g + 1) * SLAB]
            turned = mm(swap, block.reshape(SLAB * SLAB, channels))
            start = base + c * SLAB
            out_ref[g * SLAB : (g + 1) * SLAB, start : start + SLAB] = turned.astype(
                BF16
            ).reshape(SLAB, SLAB, channels)


def gather_bias(block, groups):
    if groups != 8:
        return lax.all_gather(block, "res", axis=0, tiled=False)
    side, lines = 2, groups // 2
    here = lax.axis_index("res")
    across = lax.ppermute(block, "res", [(i, i ^ 1) for i in range(groups)])
    odd = here % side == 1
    own = jnp.stack([jnp.where(odd, across, block), jnp.where(odd, block, across)])
    up, down = [own], [own]
    for _ in range(lines - 1):
        up.append(lax.ppermute(up[-1], "res", [(i, i + side) for i in range(groups - side)]))
        down.append(lax.ppermute(down[-1], "res", [(i, i - side) for i in range(side, groups)]))
    line = here // side
    pairs = []
    for at in range(lines):
        pairs.append(
            lax.select_n(line, *[up[z - at] if z >= at else down[at - z] for z in range(lines)])
        )
    return jnp.concatenate(pairs, axis=0)


def in_vmem(count):
    return [pl.BlockSpec(memory_space=pltpu.VMEM)] * count


def anywhere(count):
    return [pl.BlockSpec(memory_space=pl.ANY)] * count


def like(*arrays):
    return [pltpu.VMEM(array.shape, array.dtype) for array in arrays]


def body(
    aligned_chain_features,
    pair_representation_state,
    gap_block_flags,
    pair_norm_gain,
    pair_head_weight,
    horizontal_scaling_factor,
    row_input_weight,
    horizontal_final_matrix,
    vertical_scaling_factor,
    column_input_weight,
    vertical_final_matrix,
    feedforward_scaling_factor,
    feedforward_widen_matrix,
    feedforward_shrink_matrix,
):
    groups = lax.axis_size("res")
    total_seqs, local_res, channels = aligned_chain_features.shape
    residues = pair_representation_state.shape[1]
    heads = pair_head_weight.shape[1]
    local_seqs = total_seqs // groups
    turn = local_res % SLAB == 0
    res_parts = local_res // SLAB if turn else 1
    part_res = local_res // res_parts
    here = lax.axis_index("res")

    def exchange(values):
        return lax.all_to_all(values, "res", split_axis=0, concat_axis=0, tiled=True)

    def kernel_call(kernel, name, micros, in_specs, out_shape, scratch):
        return pl.pallas_call(
            kernel,
            out_shape=jax.ShapeDtypeStruct(out_shape, BF16),
            in_specs=in_specs,
            out_specs=pl.BlockSpec(memory_space=pltpu.VMEM),
            scratch_shapes=scratch,
            compiler_params=pltpu.CompilerParams(vmem_limit_bytes=VMEM_BYTES),
            cost_estimate=pl.CostEstimate(
                flops=int(micros * 1e9), bytes_accessed=1 << 20, transcendentals=0
            ),
            name=name,
        )

    arrived = exchange(
        aligned_chain_features.reshape(groups, local_seqs, local_res, channels)
    )
    bias_local = kernel_call(
        bias_kernel, "pair_bias", 5, in_vmem(3), (heads, local_res, residues),
        [pltpu.VMEM((local_res, heads, residues), F32)],
    )(pair_representation_state, pair_norm_gain[None, :], pair_head_weight.T)
    bias_all = gather_bias(bias_local, groups)

    def slots(weight):
        return [weight[:, i * channels : (i + 1) * channels] for i in range(4)]

    rq, rk, rv, rg = slots(row_input_weight)
    row_weights = (rk, rv.T, jnp.concatenate([rq, rg], axis=1).T, horizontal_final_matrix)
    cq, ck, cv, cg = slots(column_input_weight)
    col_weights = (
        ck, jnp.concatenate([cq, cv, cg], axis=1).T, vertical_final_matrix,
        feedforward_widen_matrix, feedforward_shrink_matrix,
    )
    gap = lax.dynamic_slice_in_dim(gap_block_flags, here * local_seqs, local_seqs, 0)
    column_block = (here * local_res) // BLOCK
    col_gap = lax.dynamic_slice_in_dim(gap_block_flags, column_block, 1, 1)

    def row_attention(low, count):
        queries = groups * count
        operands = (arrived, *row_weights, bias_all)
        return kernel_call(
            functools.partial(row_kernel, low, count), "row_attention", 10,
            [pl.BlockSpec(memory_space=pltpu.SMEM)] + in_vmem(1) + anywhere(6),
            (groups, local_seqs, count, channels),
            like(*operands)
            + [
                pltpu.SemaphoreType.DMA((6,)),
                pltpu.VMEM((heads + 1, residues, queries), F32),
                pltpu.VMEM((local_seqs, channels, queries), BF16),
                pltpu.VMEM((local_seqs, residues, channels), BF16),
                pltpu.VMEM((local_seqs, channels, residues), BF16),
                pltpu.VMEM((local_seqs, channels, queries), F32),
                pltpu.VMEM((local_seqs, queries, channels), BF16),
            ],
        )(gap, horizontal_scaling_factor[None, :], *operands)

    finals = [exchange(row_attention(c * part_res, part_res)) for c in range(res_parts)]
    done = []
    for c in range(res_parts):
        piece = finals[c].reshape(total_seqs, part_res, channels)
        if not turn:
            piece = jnp.swapaxes(piece, 0, 1)
        before = done if c == res_parts - 1 else []
        if not turn:
            shape = (part_res, total_seqs, channels)
        else:
            shape = (total_seqs, part_res * (1 + len(before)), channels)
        operands = (piece, *col_weights)
        done.append(
            kernel_call(
                functools.partial(column_kernel, heads, turn, len(before)),
                "column_transition", 10,
                in_vmem(3) + anywhere(6) + in_vmem(len(before)), shape,
                like(*operands)
                + [
                    pltpu.SemaphoreType.DMA((6,)),
                    pltpu.VMEM((part_res, total_seqs, channels), BF16),
                    pltpu.VMEM((part_res, channels, total_seqs), BF16),
                    pltpu.VMEM((part_res, total_seqs, channels), BF16),
                    pltpu.VMEM((part_res, channels, total_seqs), BF16),
                    pltpu.VMEM((part_res, channels, total_seqs), F32),
                    pltpu.VMEM((part_res, total_seqs, channels), BF16),
                    pltpu.VMEM((part_res, total_seqs, channels), BF16),
                ],
            )(
                col_gap, vertical_scaling_factor[None, :], feedforward_scaling_factor[None, :],
                *operands, *before,
            )
        )
    return done[-1] if turn else jnp.swapaxes(done[-1], 0, 1)


def solution(mesh):
    placed = (
        P("dp", "res", None),
        P(("dp", "res"), None, None),
        P("dp", None),
    ) + (P(),) * 11
    return jax.shard_map(
        body, mesh=mesh, in_specs=placed, out_specs=P("dp", "res", None), check_vma=False
    )
```

time: 210 us -> 196 us (0.933)
  blocking collectives: 18.4 us -> 0 us
  waiting for transfers between devices: 17.8 us -> 30.6 us
  Pallas kernels: 102 us -> 90.4 us
  starting transfers between devices: 46.3 us -> 53.8 us
  local copies, waits for them, and re-layouts: 22.7 us -> 18.7 us
    all_to_all x1 -> x0, blocking collectives: 18.4 us -> none  [exchange(): lax.all_to_all(values, 'res', split_axis=0, concat_axis=0, tiled=True)]
    ppermute x3, starting transfers between devices: 16.8 us -> 28.2 us  [gather_bias(): lax.ppermute(up[-1], 'res', [(i, i + side) for i in range(groups - side)])]
    pallas_call x6 -> x5, Pallas kernels: 102 us -> 90.4 us  [the longest x2 43.6 us: row_attention(): kernel_call(functools.partial(row_kernel, low, count), 'row_attention', 1...]
    ppermute x3, waiting for transfers between devices: 0.01 us -> 9.05 us  [gather_bias(): lax.ppermute(down[-1], 'res', [(i, i - side) for i in range(side, groups)])]
    ppermute x1, waiting for transfers between devices: 7.06 us -> 13.1 us  [gather_bias(): across = lax.ppermute(block, 'res', [(i, i ^ 1) for i in range(groups)])]
    slice x3 -> x4, local copies, waits for them, and re-layouts: 6.72 us -> 1.35 us  [slots(): return [weight[:, i * channels:(i + 1) * channels] for i in range(4)]]
    all_to_all x4 -> x3, starting transfers between devices: 23.6 us -> 19.7 us  [exchange(): lax.all_to_all(values, 'res', split_axis=0, concat_axis=0, tiled=True)]
    unnamed x61 -> x65, local copies, waits for them, and re-layouts: 15.9 us -> 17.3 us
  transfers between devices with their start and end apart: 11 -> 10, of which waited for: 5 -> 6; matrix products, arithmetic and copies ran while one was open for 4% -> 2% of each run, Pallas kernels for 30% -> 24%
where the time goes in v1:
time: 196 us; the launch traced here: 195 us
  Pallas kernels  90.4 us (46%)
  starting transfers between devices  53.8 us (27%)
  waiting for transfers between devices  30.6 us (16%)
  local copies, waits for them, and re-layouts  18.7 us (10%)
    pallas_call x2, Pallas kernels, row_attention(): kernel_call(functools.partial(row_kernel, low, count), 'row_attention', 1...  43.6 us
    pallas_call x2, Pallas kernels, body(): kernel_call(functools.partial(column_kernel, heads, turn, len(before)), '...  42.8 us
    ppermute x3, starting transfers between devices, gather_bias(): lax.ppermute(up[-1], 'res', [(i, i + side) for i in range(groups - side)])  28.2 us
    all_to_all x3, starting transfers between devices, exchange(): lax.all_to_all(values, 'res', split_axis=0, concat_axis=0, tiled=True)  19.7 us
    unnamed x65, local copies, waits for them, and re-layouts  17.3 us
    ppermute x1, waiting for transfers between devices, gather_bias(): across = lax.ppermute(block, 'res', [(i, i ^ 1) for i in range(groups)])  13.1 us
    ppermute x3, waiting for transfers between devices, gather_bias(): lax.ppermute(down[-1], 'res', [(i, i - side) for i in range(side, groups)])  9.05 us
    ppermute x3, waiting for transfers between devices, gather_bias(): lax.ppermute(up[-1], 'res', [(i, i + side) for i in range(groups - side)])  8.35 us
  transfers between devices with their start and end apart: 10, of which 6 were waited for; matrix products, arithmetic and copies ran while one was open for 2% of the time, Pallas kernels for 24%

profile of v1, /device:TPU:0, one launch (start us, length us, event | category | flops | bytes accessed | tf_op | source)
XLA Modules:
  0.0 195.5 jit_solution(14316695425425268029)
XLA Ops:
  0.0 7.4 %all-to-all-start = ((bf16[8,16,32,256]{3,2,1,0:T(8,128)(2,1)}), bf16[8,16,32,256]{3,2,1,0:T(8,128)(2,1)S(1)}, u32[]{:S(2)}, u32[]{:S(2)}) async-start(bf16[8,16,32,256]{3,2,1,0:T(8,128)(2,1)} %bitcast.28), calls=%async_computation | async-start | bytes 4194304 | tf_op jit(solution)/shard_map/all_to_all | solution.py:380
  7.5 1.6 copy-done.11
  9.0 4.0 %pair_bias.1 = bf16[8,32,256]{2,1,0:T(8,128)(2,1)S(1)} custom-call(bf16[32,256,128]{2,1,0:T(8,128)(2,1)S(1)} %copy-done.11, f32[1,128]{1,0:T(1,128)S(1)} %bitcast.27, bf16[8,128]{1,0:T(8,128)(2,1)S(1)} %bitcast.20), custom_call_target="tpu_custom_call" | custom-call | flops 5000000000 | bytes 1048576 | tf_op jit(solution)/shard_map/pair_bias/pallas_call | solution.py:399
  13.0 2.1 %collective-permute-start = (bf16[8,32,256]{2,1,0:T(8,128)(2,1)S(1)}, bf16[8,32,256]{2,1,0:T(8,128)(2,1)S(1)}, u32[]{:S(2)}, u32[]{:S(2)}) collective-permute-start(bf16[8,32,256]{2,1,0:T(8,128)(2,1)S(1)} %pair_bias.1), channel_id=1, source_target_pairs={{0,4},{4,0},{8,12},{12,8},{16,20},{20,16},{24,28},{28,24},{1,5},{5... | collective-permute-start | bytes 393224 | tf_op jit(solution)/shard_map/ppermute | solution.py:325
  15.1 13.1 %collective-permute-done = bf16[8,32,256]{2,1,0:T(8,128)(2,1)S(1)} collective-permute-done((bf16[8,32,256]{2,1,0:T(8,128)(2,1)S(1)}, bf16[8,32,256]{2,1,0:T(8,128)(2,1)S(1)}, u32[]{:S(2)}, u32[]{:S(2)}) %collective-permute-start) | collective-permute-done | bytes 131104 | tf_op jit(solution)/shard_map/ppermute | solution.py:325
  28.3 1.3 collective-permute-start.4
  29.6 4.6 %collective-permute-start.1 = (bf16[2,8,32,256]{3,2,1,0:T(8,128)(2,1)S(1)}, bf16[2,8,32,256]{3,2,1,0:T(8,128)(2,1)S(1)}, u32[]{:S(2)}, u32[]{:S(2)}) collective-permute-start(bf16[2,8,32,256]{3,2,1,0:T(8,128)(2,1)S(1)} %pad_maximum_fusion.1), channel_id=1, source_target_pairs={{0,8},{4,12},{8,16},{12,20},{16,24},{20,28},{1,9},{5,13},{9,17},{1... | collective-permute-start | bytes 786440 | tf_op jit(solution)/shard_map/ppermute | solution.py:330
  34.2 5.7 %collective-permute-done.4 = bf16[2,8,32,256]{3,2,1,0:T(8,128)(2,1)S(1)} collective-permute-done((bf16[2,8,32,256]{3,2,1,0:T(8,128)(2,1)S(1)}, bf16[2,8,32,256]{3,2,1,0:T(8,128)(2,1)S(1)}, u32[]{:S(2)}, u32[]{:S(2)}) %collective-permute-start.4) | collective-permute-done | bytes 262176 | tf_op jit(solution)/shard_map/ppermute | solution.py:331
  39.9 1.3 collective-permute-start.5
  41.2 6.9 %collective-permute-done.1 = bf16[2,8,32,256]{3,2,1,0:T(8,128)(2,1)S(1)} collective-permute-done((bf16[2,8,32,256]{3,2,1,0:T(8,128)(2,1)S(1)}, bf16[2,8,32,256]{3,2,1,0:T(8,128)(2,1)S(1)}, u32[]{:S(2)}, u32[]{:S(2)}) %collective-permute-start.1) | collective-permute-done | bytes 262176 | tf_op jit(solution)/shard_map/ppermute | solution.py:330
  48.0 18.4 %collective-permute-start.2 = (bf16[2,8,32,256]{3,2,1,0:T(8,128)(2,1)S(1)}, bf16[2,8,32,256]{3,2,1,0:T(8,128)(2,1)}, u32[]{:S(2)}, u32[]{:S(2)}) collective-permute-start(bf16[2,8,32,256]{3,2,1,0:T(8,128)(2,1)S(1)} %collective-permute-done.1), channel_id=1, source_target_pairs={{0,8},{4,12},{8,16},{12,20},{16,24},{20,28},{1,9},{5,13},{9,17},{1... | collective-permute-start | bytes 786440 | tf_op jit(solution)/shard_map/ppermute | solution.py:330
  66.6 2.4 %collective-permute-done.5 = bf16[2,8,32,256]{3,2,1,0:T(8,128)(2,1)} collective-permute-done((bf16[2,8,32,256]{3,2,1,0:T(8,128)(2,1)S(1)}, bf16[2,8,32,256]{3,2,1,0:T(8,128)(2,1)}, u32[]{:S(2)}, u32[]{:S(2)}) %collective-permute-start.5) | collective-permute-done | bytes 262176 | tf_op jit(solution)/shard_map/ppermute | solution.py:331
  69.0 1.3 collective-permute-start.6
  70.3 5.3 %collective-permute-start.3 = (bf16[2,8,32,256]{3,2,1,0:T(8,128)(2,1)}, bf16[2,8,32,256]{3,2,1,0:T(8,128)(2,1)}, u32[]{:S(2)}, u32[]{:S(2)}) collective-permute-start(bf16[2,8,32,256]{3,2,1,0:T(8,128)(2,1)} %collective-permute-done.2), channel_id=1, source_target_pairs={{0,8},{4,12},{8,16},{12,20},{16,24},{20,28},{1,9},{5,13},{9,17},{1... | collective-permute-start | bytes 786440 | tf_op jit(solution)/shard_map/ppermute | solution.py:330
  76.7 0.9 collective-permute-done.6
  77.6 1.5 collective-permute-done.3
  79.1 1.4 select_select_fusion.3
  80.7 1.1 copy-done.7
  81.7 0.9 copy-done.16
  82.6 21.8 %row_attention.3 = bf16[8,16,16,256]{3,2,1,0:T(8,128)(2,1)S(1)} custom-call(s32[16,2]{1,0:T(8,128)S(1)} %copy.23.gap_ref, f32[1,256]{1,0:T(1,128)S(1)} %bitcast.21, bf16[8,16,32,256]{3,2,1,0:T(8,128)(2,1)S(1)} %all-to-all-done.x_hbm, bf16[256,256]{1,0:T(8,128)(2,1)S(1)} %copy-done.7, bf16[256,256]{1,0:T(8,128)(2,1)S(1)} %bitcast.18, ...), custom_call_target="tpu_custom_call" | custom-call | flops 10000000000 | bytes 1048576 | tf_op jit(solution)/shard_map/row_attention/pallas_call | solution.py:422
  104.4 1.0 copy-done.4
  105.4 6.1 %all-to-all-start.2 = ((bf16[8,16,16,256]{3,2,1,0:T(8,128)(2,1)}), bf16[8,16,16,256]{3,2,1,0:T(8,128)(2,1)S(1)}, u32[]{:S(2)}, u32[]{:S(2)}) async-start(bf16[8,16,16,256]{3,2,1,0:T(8,128)(2,1)} %copy-done.4), calls=%async_computation.2 | async-start | bytes 2097152 | tf_op jit(solution)/shard_map/all_to_all | solution.py:380
  111.6 1.2 copy-done.3
  112.8 0.9 copy-done.8
  114.6 21.8 %row_attention.2 = bf16[8,16,16,256]{3,2,1,0:T(8,128)(2,1)S(1)} custom-call(s32[16,2]{1,0:T(8,128)S(1)} %copy.23.gap_ref, f32[1,256]{1,0:T(1,128)S(1)} %bitcast.22, bf16[8,16,32,256]{3,2,1,0:T(8,128)(2,1)S(1)} %all-to-all-done.x_hbm, bf16[256,256]{1,0:T(8,128)(2,1)S(1)} %copy-done.8, bf16[256,256]{1,0:T(8,128)(2,1)S(1)} %bitcast.19, ...), custom_call_target="tpu_custom_call" | custom-call | flops 10000000000 | bytes 1048576 | tf_op jit(solution)/shard_map/row_attention/pallas_call | solution.py:422
  136.4 1.0 copy-done.1
  137.4 6.1 %all-to-all-start.1 = ((bf16[8,16,16,256]{3,2,1,0:T(8,128)(2,1)}), bf16[8,16,16,256]{3,2,1,0:T(8,128)(2,1)}, u32[]{:S(2)}, u32[]{:S(2)}) async-start(bf16[8,16,16,256]{3,2,1,0:T(8,128)(2,1)} %copy-done.1), calls=%async_computation.1 | async-start | bytes 2097152 | tf_op jit(solution)/shard_map/all_to_all | solution.py:380
  147.0 0.9 copy-done.18
  147.9 20.5 %column_transition.2.refs_0_ = bf16[128,16,256]{2,1,0:T(8,128)(2,1)S(1)} custom-call(s32[128,1]{1,0:T(8,128)S(1)} %copy-done.9, f32[1,256]{1,0:T(1,128)S(1)} %bitcast.23, f32[1,256]{1,0:T(1,128)S(1)} %bitcast.25, bf16[128,16,256]{2,1,0:T(8,128)(2,1)S(1)} %bitcast.17, bf16[256,256]{1,0:T(8,128)(2,1)S(1)} %copy-done.5, ...), custom_call_target="tpu_custom_call" | custom-call | flops 10000000000 | bytes 1048576 | tf_op jit(solution)/shard_map/column_transition/pallas_call | solution.py:451
  170.2 1.0 copy-done.13
  171.2 1.0 copy-done.15
  173.2 22.3 %column_transition.3 = bf16[128,32,256]{2,1,0:T(8,128)(2,1)} custom-call(s32[128,1]{1,0:T(8,128)S(1)} %copy-done.10, f32[1,256]{1,0:T(1,128)S(1)} %bitcast.24, f32[1,256]{1,0:T(1,128)S(1)} %bitcast.26, bf16[128,16,256]{2,1,0:T(8,128)(2,1)} %bitcast.10.x_hbm, bf16[256,256]{1,0:T(8,128)(2,1)S(1)} %copy-done.6, ...), custom_call_target="tpu_custom_call" | custom-call | flops 10000000000 | bytes 1048576 | tf_op jit(solution)/shard_map/column_transition/pallas_call | solution.py:451
  (70 shorter events, 8.4 us)
Async XLA Ops:
  0.0 66.4 %copy-start = (s32[128,2]{0,1:T(2,128)S(1)}, s32[128,2]{0,1:T(2,128)}, u32[]{:S(2)}) copy-start(s32[128,2]{0,1:T(2,128)} %param.16) | copy-start | bytes 3076
  0.0 7.4 %copy-start.20 = (bf16[128,8]{0,1:T(8,128)(2,1)S(1)}, bf16[128,8]{0,1:T(8,128)(2,1)}, u32[]{:S(2)}) copy-start(bf16[128,8]{0,1:T(8,128)(2,1)} %param.18) | copy-start | bytes 6148
  0.0 7.4 %copy-start.24 = (f32[128]{0:T(128)S(1)}, f32[128]{0:T(128)}, u32[]{:S(2)}) copy-start(f32[128]{0:T(128)} %param.17) | copy-start | bytes 1540
  0.0 80.7 %all-to-all-start = ((bf16[8,16,32,256]{3,2,1,0:T(8,128)(2,1)}), bf16[8,16,32,256]{3,2,1,0:T(8,128)(2,1)S(1)}, u32[]{:S(2)}, u32[]{:S(2)}) async-start(bf16[8,16,32,256]{3,2,1,0:T(8,128)(2,1)} %bitcast.28), calls=%async_computation | async-start | bytes 4194304 | tf_op jit(solution)/shard_map/all_to_all | solution.py:380
  7.5 1.6 copy-start.11
  9.0 66.6 %copy-start.26 = (bf16[256,1024]{1,0:T(8,128)(2,1)S(1)}, bf16[256,1024]{1,0:T(8,128)(2,1)}, u32[]{:S(2)}) copy-start(bf16[256,1024]{1,0:T(8,128)(2,1)} %param.20) | copy-start | bytes 1572868
  13.0 15.2 %collective-permute-start = (bf16[8,32,256]{2,1,0:T(8,128)(2,1)S(1)}, bf16[8,32,256]{2,1,0:T(8,128)(2,1)S(1)}, u32[]{:S(2)}, u32[]{:S(2)}) collective-permute-start(bf16[8,32,256]{2,1,0:T(8,128)(2,1)S(1)} %pair_bias.1), channel_id=1, source_target_pairs={{0,4},{4,0},{8,12},{12,8},{16,20},{20,16},{24,28},{28,24},{1,5},{5... | collective-permute-start | bytes 393224 | tf_op jit(solution)/shard_map/ppermute | solution.py:325
  28.3 11.6 %collective-permute-start.4 = (bf16[2,8,32,256]{3,2,1,0:T(8,128)(2,1)S(1)}, bf16[2,8,32,256]{3,2,1,0:T(8,128)(2,1)S(1)}, u32[]{:S(2)}, u32[]{:S(2)}) collective-permute-start(bf16[2,8,32,256]{3,2,1,0:T(8,128)(2,1)S(1)} %pad_maximum_fusion.1), channel_id=1, source_target_pairs={{8,0},{12,4},{16,8},{20,12},{24,16},{28,20},{9,1},{13,5},{17,9},{2... | collective-permute-start | bytes 786440 | tf_op jit(solution)/shard_map/ppermute | solution.py:331
  29.6 18.4 %collective-permute-start.1 = (bf16[2,8,32,256]{3,2,1,0:T(8,128)(2,1)S(1)}, bf16[2,8,32,256]{3,2,1,0:T(8,128)(2,1)S(1)}, u32[]{:S(2)}, u32[]{:S(2)}) collective-permute-start(bf16[2,8,32,256]{3,2,1,0:T(8,128)(2,1)S(1)} %pad_maximum_fusion.1), channel_id=1, source_target_pairs={{0,8},{4,12},{8,16},{12,20},{16,24},{20,28},{1,9},{5,13},{9,17},{1... | collective-permute-start | bytes 786440 | tf_op jit(solution)/shard_map/ppermute | solution.py:330
  39.9 30.4 %copy-start.27 = (bf16[2,8,32,256]{3,2,1,0:T(8,128)(2,1)}, bf16[2,8,32,256]{3,2,1,0:T(8,128)(2,1)S(1)}, u32[]{:S(2)}) copy-start(bf16[2,8,32,256]{3,2,1,0:T(8,128)(2,1)S(1)} %collective-permute-done.4) | copy-start | bytes 786436
  39.9 29.1 %collective-permute-start.5 = (bf16[2,8,32,256]{3,2,1,0:T(8,128)(2,1)S(1)}, bf16[2,8,32,256]{3,2,1,0:T(8,128)(2,1)}, u32[]{:S(2)}, u32[]{:S(2)}) collective-permute-start(bf16[2,8,32,256]{3,2,1,0:T(8,128)(2,1)S(1)} %collective-permute-done.4), channel_id=1, source_target_pairs={{8,0},{12,4},{16,8},{20,12},{24,16},{28,20},{9,1},{13,5},{17,9},{2... | collective-permute-start | bytes 786440 | tf_op jit(solution)/shard_map/ppermute | solution.py:331
  48.0 22.3 %copy-start.28 = (bf16[2,8,32,256]{3,2,1,0:T(8,128)(2,1)}, bf16[2,8,32,256]{3,2,1,0:T(8,128)(2,1)S(1)}, u32[]{:S(2)}) copy-start(bf16[2,8,32,256]{3,2,1,0:T(8,128)(2,1)S(1)} %collective-permute-done.1) | copy-start | bytes 786436
  48.0 22.3 %collective-permute-start.2 = (bf16[2,8,32,256]{3,2,1,0:T(8,128)(2,1)S(1)}, bf16[2,8,32,256]{3,2,1,0:T(8,128)(2,1)}, u32[]{:S(2)}, u32[]{:S(2)}) collective-permute-start(bf16[2,8,32,256]{3,2,1,0:T(8,128)(2,1)S(1)} %collective-permute-done.1), channel_id=1, source_target_pairs={{0,8},{4,12},{8,16},{12,20},{16,24},{20,28},{1,9},{5,13},{9,17},{1... | collective-permute-start | bytes 786440 | tf_op jit(solution)/shard_map/ppermute | solution.py:330
  69.0 8.6 %collective-permute-start.6 = (bf16[2,8,32,256]{3,2,1,0:T(8,128)(2,1)}, bf16[2,8,32,256]{3,2,1,0:T(8,128)(2,1)}, u32[]{:S(2)}, u32[]{:S(2)}) collective-permute-start(bf16[2,8,32,256]{3,2,1,0:T(8,128)(2,1)} %collective-permute-done.5), channel_id=1, source_target_pairs={{8,0},{12,4},{16,8},{20,12},{24,16},{28,20},{9,1},{13,5},{17,9},{2... | collective-permute-start | bytes 786440 | tf_op jit(solution)/shard_map/ppermute | solution.py:331
  70.3 8.7 %collective-permute-start.3 = (bf16[2,8,32,256]{3,2,1,0:T(8,128)(2,1)}, bf16[2,8,32,256]{3,2,1,0:T(8,128)(2,1)}, u32[]{:S(2)}, u32[]{:S(2)}) collective-permute-start(bf16[2,8,32,256]{3,2,1,0:T(8,128)(2,1)} %collective-permute-done.2), channel_id=1, source_target_pairs={{0,8},{4,12},{8,16},{12,20},{16,24},{20,28},{1,9},{5,13},{9,17},{1... | collective-permute-start | bytes 786440 | tf_op jit(solution)/shard_map/ppermute | solution.py:330
  76.6 4.0 %copy-start.21 = (f32[256]{0:T(256)S(1)}, f32[256]{0:T(256)}, u32[]{:S(2)}) copy-start(f32[256]{0:T(256)} %param.19) | copy-start | bytes 3076
  80.6 23.8 %copy-start.2 = (bf16[8,8,32,256]{3,2,1,0:T(8,128)(2,1)}, bf16[8,8,32,256]{3,2,1,0:T(8,128)(2,1)S(1)}, u32[]{:S(2)}) copy-start(bf16[8,8,32,256]{3,2,1,0:T(8,128)(2,1)S(1)} %pad_maximum_fusion.bias_hbm) | copy-start | bytes 3145732
  80.7 1.1 copy-start.7
  104.4 1.0 copy-start.4
  105.4 31.9 %all-to-all-start.2 = ((bf16[8,16,16,256]{3,2,1,0:T(8,128)(2,1)}), bf16[8,16,16,256]{3,2,1,0:T(8,128)(2,1)S(1)}, u32[]{:S(2)}, u32[]{:S(2)}) async-start(bf16[8,16,16,256]{3,2,1,0:T(8,128)(2,1)} %copy-done.4), calls=%async_computation.2 | async-start | bytes 2097152 | tf_op jit(solution)/shard_map/all_to_all | solution.py:380
  111.6 1.2 copy-start.3
  136.4 1.0 copy-start.1
  137.4 6.9 %slice-start = ((bf16[256,1024]{1,0:T(8,128)(2,1)}), bf16[256,512]{1,0:T(8,128)(2,1)S(1)}, s32[]{:S(2)}) async-start(bf16[256,1024]{1,0:T(8,128)(2,1)} %param.23), calls=%async_computation.3 | async-start | bytes 524288 | tf_op jit(solution)/shard_map/slice | solution.py:406
  137.4 7.1 %copy-start.25 = (bf16[256,1024]{1,0:T(8,128)(2,1)S(1)}, bf16[256,1024]{1,0:T(8,128)(2,1)}, u32[]{:S(2)}) copy-start(bf16[256,1024]{1,0:T(8,128)(2,1)} %param.23) | copy-start | bytes 1572868
  137.4 7.9 %copy-start.12 = (bf16[256,1024]{1,0:T(8,128)(2,1)S(1)}, bf16[256,1024]{1,0:T(8,128)(2,1)}, u32[]{:S(2)}) copy-start(bf16[256,1024]{1,0:T(8,128)(2,1)} %widen_hbm.3) | copy-start | bytes 1572868
  137.4 7.9 %copy-start.14 = (bf16[1024,256]{1,0:T(8,128)(2,1)S(1)}, bf16[1024,256]{1,0:T(8,128)(2,1)}, u32[]{:S(2)}) copy-start(bf16[1024,256]{1,0:T(8,128)(2,1)} %shrink_hbm.3) | copy-start | bytes 1572868
  137.4 7.9 %copy-start.22 = (f32[256]{0:T(256)S(1)}, f32[256]{0:T(256)}, u32[]{:S(2)}) copy-start(f32[256]{0:T(256)} %param.22) | copy-start | bytes 3076
  137.4 7.9 %copy-start.23 = (f32[256]{0:T(256)S(1)}, f32[256]{0:T(256)}, u32[]{:S(2)}) copy-start(f32[256]{0:T(256)} %param.25) | copy-start | bytes 3076
  137.4 31.0 %all-to-all-start.1 = ((bf16[8,16,16,256]{3,2,1,0:T(8,128)(2,1)}), bf16[8,16,16,256]{3,2,1,0:T(8,128)(2,1)}, u32[]{:S(2)}, u32[]{:S(2)}) async-start(bf16[8,16,16,256]{3,2,1,0:T(8,128)(2,1)} %copy-done.1), calls=%async_computation.1 | async-start | bytes 2097152 | tf_op jit(solution)/shard_map/all_to_all | solution.py:380
  145.3 0.9 copy-start.5
  170.2 1.0 copy-start.13
  171.2 1.0 copy-start.15
  (8 other events, 7.1 us)
